TPU v7x, 128 devices: a whole 4x4x4 slice. The times are simulated.
128 devices in a mesh: row: 16 (over x, z), col: 8 (over y, core).
Axes of the slice: x: 4, y: 4, z: 4, core: 2. Of those that a mesh axis runs over, the one named last changes fastest.
Arguments:
- tokens: bfloat16 [16384, 8192], P('row', 'col'), may hold values from -6 to 6
- weights: bfloat16 [4, 112, 128, 256], P(None, 'col', 'row'), may hold values from -0.25 to 0.25
- block_rows: int32 [4, 112], P(None, 'col'), may hold values from 0 to 63, as said below
- grad_hidden: bfloat16 [16384, 14336], P('row', 'col'), may hold values from -6 to 6
Outputs:
- hidden: bfloat16 [16384, 14336], P(('row', 'col'))
- grad_tokens: bfloat16 [16384, 8192], P(('row', 'col'))
- grad_weights: bfloat16 [4, 112, 128, 256], P(None, 'col', 'row')
Inputs may be any that keep to these rules, and one draw needn't show every extreme that they name: `block_rows`: block row indices; an index may appear more than once in a block column, and then both blocks add.
All inputs are finite; a program needn't handle non-finite values.
Results may differ from a plain program's by a relative error of at most 0.018.
Values may be sent and summed in bfloat16 or wider, within the bound.
A program may use at most 192 MiB of HBM per device.

v0:
```python
import jax
import jax.numpy as jnp
from jax import lax
from jax.experimental import pallas as pl
from jax.experimental.pallas import tpu as pltpu
from jax.sharding import PartitionSpec as P

MESH = pl.DeviceIdType.MESH
BF, F32 = jnp.bfloat16, jnp.float32
HBM = pl.BlockSpec(memory_space=pltpu.HBM)
WIRES, LOCALS = 88, 24
VMEM = pl.BlockSpec(memory_space=pltpu.VMEM)


def place():
    row, col = lax.axis_index("row"), lax.axis_index("col")
    return row // 4, row % 4, col // 2, col % 2


def at(x, z, y, core):
    return (x * 4 + z, y * 2 + core)


def greet(peers):
    barrier = pltpu.get_barrier_semaphore()
    for peer in peers:
        pl.semaphore_signal(barrier, inc=1, device_id=peer, device_id_type=MESH)
    pl.semaphore_wait(barrier, len(peers))


class Wires:
    def __init__(self, send, recv):
        self.send, self.recv, self.made = send, recv, 0
        self.unsent, self.ungot = [], []

    def copy(self, src, dst, peer):
        i = self.made
        self.made += 1
        c = pltpu.make_async_remote_copy(
            src_ref=src,
            dst_ref=dst,
            send_sem=self.send.at[i],
            recv_sem=self.recv.at[i],
            device_id=peer,
            device_id_type=MESH,
        )
        c.start()
        self.unsent.append(c)
        self.ungot.append(c)
        return c

    def sent(self, *copies):
        for c in copies:
            self.unsent = [o for o in self.unsent if o is not c]
            c.wait_send()

    def got(self, *copies):
        for c in copies:
            self.ungot = [o for o in self.ungot if o is not c]
            c.wait_recv()

    def finish(self):
        self.got(*list(self.ungot))
        self.sent(*list(self.unsent))


def weight_terms(half, columns, br_ref, tok, own_w, gh, picked, grads, acc, dw):
    def column(j, _):
        rows = [br_ref[k, j] for k in range(4)]
        wide = jnp.concatenate(
            [own_w[k // 2, k % 2, j].reshape(128, 256) for k in range(4)], axis=0
        )
        lane = pl.ds(pl.multiple_of(j * 128, 128), 128)
        for k in range(4):
            picked[:, k * 128 : k * 128 + 128] = tok[rows[k]]
        for t in range(2):
            span = slice(t * 256, t * 256 + 256)
            joined = dot(picked[span], wide, ((1,), (0,)))
            grad = gh[pl.ds(half * 512 + t * 256, 256), lane].astype(F32)
            _, grad_gate, grad_up = swish_parts(joined, grad)
            grads[span, :128] = grad_gate
            grads[span, 128:] = grad_up
        term = dot(picked[...], grads[...], ((0,), (0,)))
        if half == 0:
            acc[j] = term
        else:
            total = (acc[j] + term).astype(BF).reshape(4, 4, 2, 16, 256)
            for k in range(4):
                dw[k // 2, k % 2, j] = total[k]
        return 0

    lax.fori_loop(columns[0], columns[1], column, 0)


def gather_kernel(
    tok_ref, wv_ref, gh_ref, br_ref, rows_ref,
    tokb, wide, ghb, brb, out,
    tok, tokv, wv, wp, slab, own_w, gh, picked, grads, acc, dw,
    l0, l1, s0, s1, m0, m1, swap,
    send, recv, local,
):
    x, z, y, core = place()
    col = y * 2 + core
    e, zh = z % 2, z // 2
    yp, ym, y2 = (y + 1) % 4, (y + 3) % 4, (y + 2) % 4
    zp, zm, z2 = (z + 1) % 4, (z + 3) % 4, (z + 2) % 4
    xp, xm, x2 = (x + 1) % 4, (x + 3) % 4, (x + 2) % 4
    sib = at(x, z, y, 1 - core)
    up, down = at(x, z, yp, core), at(x, z, ym, core)
    cols = [(col + d) % 8 for d in range(1, 8)]
    col_peers = [at(x, z, c // 2, c % 2) for c in cols]
    x_peers = [at(v, z, y, core) for v in (xp, xm, x2)]
    z_peers = [at(x, v, y, core) for v in (zp, zm, z2)]
    wires = Wires(send, recv)
    go, sent, got = wires.copy, wires.sent, wires.got
    locals_made = [0]

    def lcopy(src, dst):
        c = pltpu.make_async_copy(src, dst, local.at[locals_made[0]])
        locals_made[0] += 1
        c.start()
        return c

    def same(part, peer):
        return go(part, part, peer)

    staged = lcopy(tok_ref, tokv)
    own_wv = lcopy(wv_ref.at[e], wv)
    staged.wait()
    own_tok = [
        [
            lcopy(
                tokv.at[pl.ds(512 * r, 512), pl.ds(m * 128, 128)], tok[r].at[col * 8 + m]
            )
            for m in range(8)
        ]
        for r in range(2)
    ]
    own_br = lcopy(br_ref, brb.at[col])
    own_gh = lcopy(gh_ref, gh)
    own_ghb = lcopy(gh_ref.at[pl.ds(pl.multiple_of(col * 128, 128), 128)], ghb.at[col])
    greet(col_peers + x_peers + z_peers)
    pair = go(wv_ref.at[1 - e], wp, at(x, z + 1 - 2 * e, y, core))

    def shard(r, yy, cc):
        return tok[r].at[pl.ds((yy * 2 + cc) * 8, 8)]

    def half_shard(r, yy, h):
        return tok[r].at[pl.ds((yy * 2 + core) * 8 + 4 * h, 4)]

    def start_tokens(r):
        sends = [same(shard(r, y, core), p) for p in (up, down)]
        return sends, [same(shard(r, y, core), sib)]

    def forward_tokens(r, sends, shares):
        got(*sends)
        shares += [same(shard(r, v, core), sib) for v in (ym, yp)]
        return [same(half_shard(r, ym, 0), up), same(half_shard(r, yp, 1), down)]

    def finish_tokens(r, shares, forwards):
        got(*forwards)
        last = same(shard(r, y2, core), sib)
        if r == 1:
            sent(*forwards)
            for c, p in zip(cols, col_peers):
                go(gh_ref.at[pl.ds(pl.multiple_of(c * 128, 128), 128)], ghb.at[col], p)
        got(*shares)
        got(last)

    for c in own_tok[0]:
        c.wait()
    sends0, shares0 = start_tokens(0)
    for c, p in zip(cols, col_peers):
        go(br_ref, brb.at[col], p)
    own_wv.wait()
    got(pair)
    mine, other = wv[...].astype(F32), wp[...].astype(F32)
    low = jnp.where(e == 0, mine, other)
    high = jnp.where(e == 0, other, mine)
    gate = jnp.concatenate([low[:, :8], high[:, :8]], axis=1).astype(BF)
    upper = jnp.concatenate([low[:, 8:], high[:, 8:]], axis=1).astype(BF)
    slab[:, :, :, :128] = gate.reshape(2, 14, 16, 128)
    slab[:, :, :, 128:] = upper.reshape(2, 14, 16, 128)
    ystage = [
        go(slab, wide.at[(y + 4 - v) % 4, core, e, :, :, x, zh], at(x, z, v, core))
        for v in (yp, ym, y2)
    ]
    placed = lcopy(slab, wide.at[0, core, e, :, :, x, zh])
    early = [go(slab.at[0], wide.at[0, core, e, 0, :, x, zh], p) for p in x_peers]
    early += [go(slab.at[1], wide.at[0, core, e, 1, :, x, zh], p) for p in z_peers]
    placed.wait()
    got(*early)
    second = [same(wide.at[0, core, e, 0, :, :, zh], p) for p in z_peers]
    second += [same(wide.at[0, core, :, 1, :, x], p) for p in x_peers]
    got(*ystage)
    others = pl.ds(1, 3)
    first = [same(wide.at[others, core, e, 0, :, x, zh], p) for p in x_peers]
    first += [same(wide.at[others, core, e, 1, :, x, zh], p) for p in z_peers]

    for c in own_tok[1]:
        c.wait()
    forwards0 = forward_tokens(0, sends0, shares0)
    sends1, shares1 = start_tokens(1)
    got(*second)
    own_copy = lcopy(wide.at[0, core], own_w)
    got(*first)

    def w0(zz, js):
        return wide.at[others, core, zz % 2, 0, js, :, zz // 2]

    def w1(xx, js):
        return wide.at[others, core, :, 1, js, xx]

    every, lower, higher = pl.ds(0, 14), pl.ds(0, 7), pl.ds(7, 7)
    zup, zdn = at(x, zp, y, core), at(x, zm, y, core)
    xup, xdn = at(xp, z, y, core), at(xm, z, y, core)
    third = [same(w0(z, every), p) for p in (zup, zdn)] + [same(w1(x, every), p) for p in (xup, xdn)]
    for part in (w0(z, every), w1(x, every)):
        same(part, sib)
    own_copy.wait()
    same(wide.at[0, core], sib)

    finish_tokens(0, shares0, forwards0)
    forwards1 = forward_tokens(1, sends1, shares1)
    own_gh.wait()
    terms = (rows_ref, tok[0], own_w, gh, picked, grads, acc, dw)
    weight_terms(0, (0, 14), *terms)

    got(*third)
    fourth = [same(w0(zm, lower), zup), same(w0(zp, higher), zdn)]
    fourth += [same(w1(xm, lower), xup), same(w1(xp, higher), xdn)]
    for part in (w0(zm, every), w0(zp, every), w1(xm, every), w1(xp, every)):
        same(part, sib)

    finish_tokens(1, shares1, forwards1)
    rows_at = pl.ds(pl.multiple_of(col % 4 * 128, 128), 128)
    keep = [pltpu.make_async_copy(t.at[:, rows_at], tokb, local.at[LOCALS - 1]) for t in tok]
    for h in range(2):
        pl.when(col // 4 == h)(keep[h].start)
    terms = (rows_ref, tok[1], own_w, gh, picked, grads, acc, dw)
    summing = []
    for js in ((0, 7), (7, 14)):
        weight_terms(1, js, *terms)
        summing += reduce_start(wires, js, dw, l0, l1, x, z, y, core)

    got(*fourth)
    for part in (w0(z2, every), w1(x2, every)):
        same(part, sib)
    reduce_part(wires, summing, dw, out, l0, l1, s0, s1, m0, m1, swap, x, z, y, core)
    own_br.wait()
    own_ghb.wait()
    keep[0].wait()
    wires.finish()
    assert (wires.made, locals_made[0]) == (WIRES, LOCALS - 1), (wires.made, locals_made[0])


def gather_all(tokens, wv, grad_hidden, br):
    return pl.pallas_call(
        gather_body,
        out_shape=(
            jax.ShapeDtypeStruct((64, 128, 128), BF),
            jax.ShapeDtypeStruct((4, 2, 2, 2, 14, 4, 2, 16, 256), BF),
            jax.ShapeDtypeStruct((8, 128, 1792), BF),
            jax.ShapeDtypeStruct((8, 4, 14), jnp.int32),
            jax.ShapeDtypeStruct((2, 28, 16, 128), BF),
        ),
        in_specs=[HBM, HBM, HBM, HBM, pl.BlockSpec(memory_space=pltpu.SMEM)],
        out_specs=(HBM, HBM, HBM, HBM, VMEM),
        scratch_shapes=[
            pltpu.VMEM((64, 512, 128), BF),
            pltpu.VMEM((64, 512, 128), BF),
            pltpu.VMEM((1024, 1024), BF),
            pltpu.VMEM((28, 16, 128), BF),
            pltpu.VMEM((28, 16, 128), BF),
            pltpu.VMEM((2, 14, 16, 256), BF),
            pltpu.VMEM((2, 2, 14, 4, 2, 16, 256), BF),
            pltpu.VMEM((1024, 1792), BF),
            pltpu.VMEM((512, 512), BF),
            pltpu.VMEM((512, 256), BF),
            pltpu.VMEM((14, 512, 256), F32),
            pltpu.VMEM((2, 2, 14, 4, 2, 16, 256), BF),
        ]
        + REDUCE_SCRATCH
        + [
            pltpu.SemaphoreType.DMA((WIRES,)),
            pltpu.SemaphoreType.DMA((WIRES,)),
            pltpu.SemaphoreType.DMA((LOCALS,)),
        ],
        compiler_params=pltpu.CompilerParams(
            collective_id=1, has_side_effects=True, vmem_limit_bytes=60 << 20
        ),
        name="gather",
    )(tokens, wv, grad_hidden, br, br)


def gather_body(*refs):
    gather_kernel(*refs[:10], refs[10:12], *refs[12:])


def views(weights, block_rows):
    wv = weights.reshape(4, 14, 8, 2, 128).transpose(0, 1, 3, 2, 4).reshape(2, 28, 16, 128)
    return wv, block_rows


def swish_parts(joined, grad):
    gate, upper = joined[:, :128], joined[:, 128:]
    sig = 1.0 / (1.0 + jnp.exp(-gate))
    act = gate * sig
    grad_gate = grad * upper * sig * (1.0 + gate * (1.0 - sig))
    return (act * upper).astype(BF), grad_gate.astype(BF), (grad * act).astype(BF)


def dot(a, b, dims):
    return lax.dot_general(a, b, (dims, ((), ())), preferred_element_type=F32)


def tokens_kernel(me_ref, br_ref, tok_ref, w_ref, gh_ref, hid_ref, dx_ref, acc, grads):
    step = pl.program_id(0)

    @pl.when(step == 0)
    def _():
        acc[...] = jnp.zeros_like(acc)

    rows = [[br_ref[step, k, j] for k in range(4)] for j in range(14)]
    for j in range(14):
        picked = jnp.concatenate([tok_ref[i] for i in rows[j]], axis=1)
        joined = dot(picked, w_ref[0, :, j].reshape(512, 256), ((1,), (0,)))
        span = slice(j * 128, j * 128 + 128)
        hidden, grad_gate, grad_up = swish_parts(joined, gh_ref[0, :, span].astype(F32))
        hid_ref[:, span] = hidden
        grads[j, :, :128] = grad_gate
        grads[j, :, 128:] = grad_up
    for j in range(14):
        spread = dot(grads[j], w_ref[0, :, j].reshape(512, 256), ((1,), (1,)))
        for k in range(4):
            acc[rows[j][k]] += spread[:, k * 128 : k * 128 + 128]

    @pl.when(step == pl.num_programs(0) - 1)
    def _():
        for b in range(64):
            dx_ref[:, b * 128 : b * 128 + 128] = acc[b].astype(BF)


def relative(s, me, br):
    away = lax.rem(s // 2 - me[0] // 2 + 4, 4)
    return (away * 2 + s % 2, 0, 0, 0, 0)


def own_tokens(me, br, tok, wide, ghb):
    return pl.pallas_call(
        tokens_kernel,
        out_shape=(jax.ShapeDtypeStruct((128, 14336), BF), jax.ShapeDtypeStruct((128, 8192), BF)),
        grid_spec=pltpu.PrefetchScalarGridSpec(
            num_scalar_prefetch=2,
            grid=(8,),
            in_specs=[
                pl.BlockSpec((64, 128, 128), lambda s, me, br: (0, 0, 0)),
                pl.BlockSpec((1, 4, 14, 128, 256), relative),
                pl.BlockSpec((1, 128, 1792), lambda s, me, br: (s, 0, 0)),
            ],
            out_specs=(
                pl.BlockSpec((128, 1792), lambda s, me, br: (0, s)),
                pl.BlockSpec((128, 8192), lambda s, me, br: (0, 0)),
            ),
            scratch_shapes=[pltpu.VMEM((64, 128, 128), F32), pltpu.VMEM((14, 128, 256), BF)],
        ),
        compiler_params=pltpu.CompilerParams(vmem_limit_bytes=62 << 20),
        name="tokens",
    )(me, br, tok, wide, ghb)


def reduce_start(wires, columns, dw, l0, l1, x, z, y, core):
    js, made = pl.ds(columns[0], columns[1] - columns[0]), []
    for d in range(1, 4):
        zd, xd = (z + d) % 4, (x + d) % 4
        made.append(
            wires.copy(dw.at[zd % 2, 0, js, :, zd // 2], l0.at[d - 1, js], at(x, zd, y, core))
        )
        made.append(wires.copy(dw.at[:, 1, js, xd], l1.at[d - 1, :, js], at(xd, z, y, core)))
    return made


def reduce_part(wires, first, dw, out, l0, l1, s0, s1, m0, m1, swap, x, z, y, core):
    go, started = wires.copy, []
    e, zh = z % 2, z // 2
    wires.got(*first)

    def add0(j, _):
        total = dw[e, 0, j, :, zh].astype(F32)
        for d in range(3):
            total += l0[d, j].astype(F32)
        s0[j] = total.astype(BF)
        for ee in range(2):
            total = dw[ee, 1, j, x].astype(F32)
            for d in range(3):
                total += l1[d, ee, j].astype(F32)
            s1[ee, j] = total.astype(BF)
        return 0

    lax.fori_loop(0, 14, add0, 0)
    for d in range(1, 4):
        zd, xd = (z + d) % 4, (x + d) % 4
        started.append(go(s0.at[:, xd], m0.at[d - 1], at(xd, z, y, core)))
        started.append(go(s1.at[zd % 2, :, zd // 2], m1.at[d - 1], at(x, zd, y, core)))
    wires.got(*started)
    for hf in range(2):
        total = (s0[:, x] if hf == 0 else s1[e, :, zh]).astype(F32)
        got = m0 if hf == 0 else m1
        for d in range(3):
            total += got[d].astype(F32)
        low, high = total[:, :8], total[:, 8:]
        mine = jnp.where(e == 0, low, high).astype(F32)
        other = jnp.where(e == 0, high, low).astype(F32)
        span = pl.ds(14 * hf, 14)
        out[e, span] = jnp.concatenate([mine[:, :, :128], mine[:, :, 128:]], axis=1).astype(BF)
        swap[span] = jnp.concatenate([other[:, :, :128], other[:, :, 128:]], axis=1).astype(BF)
    go(swap, out.at[e], at(x, z + 1 - 2 * e, y, core))


REDUCE_SCRATCH = [
    pltpu.VMEM((3, 14, 4, 16, 256), BF),
    pltpu.VMEM((3, 2, 14, 2, 16, 256), BF),
    pltpu.VMEM((14, 4, 16, 256), BF),
    pltpu.VMEM((2, 14, 2, 16, 256), BF),
    pltpu.VMEM((3, 14, 16, 256), BF),
    pltpu.VMEM((3, 14, 16, 256), BF),
    pltpu.VMEM((28, 16, 128), BF),
]


def shards(tokens, weights, block_rows, grad_hidden):
    wv, brp = views(weights, block_rows)
    tok, wide, ghb, br, out = gather_all(tokens, wv, grad_hidden, brp)
    wide = wide.reshape(8, 4, 14, 128, 256)
    me = lax.axis_index("col").astype(jnp.int32).reshape(1)
    grad_w = out.reshape(4, 14, 2, 8, 128).transpose(0, 1, 3, 2, 4).reshape(4, 14, 8, 256)
    hidden, grad_tok = own_tokens(me, br, tok, wide, ghb)
    return hidden, grad_tok, grad_w


def solution(mesh):
    return jax.shard_map(
        shards,
        mesh=mesh,
        in_specs=(P("row", "col"), P(None, "col", "row", None), P(None, "col"), P("row", "col")),
        out_specs=(P(("row", "col"), None), P(("row", "col"), None), P(None, "col", "row", None)),
        check_vma=False,
    )
```

profile of v0, /device:TPU:0, one launch (start us, length us, event | category | flops | bytes accessed | tf_op | source)
XLA Modules:
  0.0 166.4 jit_solution(11301874595426262384)
XLA Ops:
  0.6 141.9 %gather.1 = (bf16[64,128,128]{2,1,0:T(8,128)(2,1)}, bf16[4,2,2,2,14,4,2,16,256]{8,7,6,5,4,3,2,1,0:T(8,128)(2,1)}, bf16[8,128,1792]{2,1,0:T(8,128)(2,1)}, s32[8,4,14]{2,1,0:T(4,128)}, bf16[2,28,16,128]{3,2,1,0:T(8,128)(2,1)}) custom-call(bf16[1024,1024]{1,0:T(8,128)(2,1)} %refs_0_.1, bf16[2,28,16,128]{3,2,1,0:T(8,128)(2,1)} %bitcast.14, ...), custom_call_target="tpu_custom_call" | custom-call | tf_op jit(solution)/shard_map/gather/pallas_call | solution.py:258
  142.5 0.0 copy-start
  142.5 23.2 %tokens.1 = (bf16[128,14336]{1,0:T(8,128)(2,1)}, bf16[128,8192]{1,0:T(8,128)(2,1)}) custom-call(s32[1]{0:T(128)} %bitcast.me_ref, s32[8,4,14]{2,1,0:T(4,128)} %get-tuple-element.10.br_ref, bf16[64,128,128]{2,1,0:T(8,128)(2,1)} %get-tuple-element.11.tok_ref, bf16[8,4,14,128,256]{4,3,2,1,0:T(8,128)(2,1)} %bitcast.12, ...), custom_call_target="tpu_custom_call" | custom-call | tf_op jit(solution)/shard_map/tokens/pallas_call | solution.py:350
  165.7 0.0 copy-done
  165.7 0.7 copy.8
Async XLA Ops:
  142.5 23.2 %copy-start = (bf16[2,28,16,128]{3,2,1,0:T(8,128)(2,1)S(1)}, bf16[2,28,16,128]{3,2,1,0:T(8,128)(2,1)}, u32[]{:S(2)}) copy-start(bf16[2,28,16,128]{3,2,1,0:T(8,128)(2,1)} %get-tuple-element.16) | copy-start | bytes 688132
where the time goes:
time: 167 us; the launch traced here: 166 us
  Pallas kernels  165 us (99%)
    pallas_call x1, Pallas kernels, gather_all(): pl.pallas_call(gather_body, out_shape=(jax.ShapeDtypeStruct((64, 128, 128...  142 us
    pallas_call x1, Pallas kernels, own_tokens(): pl.pallas_call(tokens_kernel, out_shape=(jax.ShapeDtypeStruct((128, 14336...  23.2 us

commit v1 on v0

--- a/solution.py
+++ b/solution.py
@@ -322,18 +322,30 @@
         acc[...] = jnp.zeros_like(acc)
 
     rows = [[br_ref[step, k, j] for k in range(4)] for j in range(14)]
+
+    def forward(j):
+        picked = jnp.concatenate([tok_ref[i] for i in rows[j]], axis=1)
+        return dot(picked, w_ref[0, :, j].reshape(512, 256), ((1,), (0,)))
+
+    def backward(j):
+        spread = dot(grads[j], w_ref[0, :, j].reshape(512, 256), ((1,), (1,)))
+        for k in range(4):
+            acc[rows[j][k]] += spread[:, k * 128 : k * 128 + 128]
+
+    following = forward(0)
     for j in range(14):
-        picked = jnp.concatenate([tok_ref[i] for i in rows[j]], axis=1)
-        joined = dot(picked, w_ref[0, :, j].reshape(512, 256), ((1,), (0,)))
+        joined = following
+        if j < 13:
+            following = forward(j + 1)
         span = slice(j * 128, j * 128 + 128)
         hidden, grad_gate, grad_up = swish_parts(joined, gh_ref[0, :, span].astype(F32))
         hid_ref[:, span] = hidden
         grads[j, :, :128] = grad_gate
         grads[j, :, 128:] = grad_up
-    for j in range(14):
-        spread = dot(grads[j], w_ref[0, :, j].reshape(512, 256), ((1,), (1,)))
-        for k in range(4):
-            acc[rows[j][k]] += spread[:, k * 128 : k * 128 + 128]
+        if j >= 2:
+            backward(j - 2)
+    backward(12)
+    backward(13)
 
     @pl.when(step == pl.num_programs(0) - 1)
     def _():

time: 167 us -> 166 us (level)
  no operation moved by 1% of the time
where the time goes in v1:
time: 166 us; the launch traced here: 165 us
  Pallas kernels  164 us (99%)
    pallas_call x1, Pallas kernels, gather_all(): pl.pallas_call(gather_body, out_shape=(jax.ShapeDtypeStruct((64, 128, 128...  142 us
    pallas_call x1, Pallas kernels, own_tokens(): pl.pallas_call(tokens_kernel, out_shape=(jax.ShapeDtypeStruct((128, 14336...  22.2 us

profile of v1, /device:TPU:0, one launch (start us, length us, event | category | flops | bytes accessed | tf_op | source)
XLA Modules:
  0.0 165.5 jit_solution(14539339696912772769)
XLA Ops:
  0.6 141.9 %gather.1 = (bf16[64,128,128]{2,1,0:T(8,128)(2,1)}, bf16[4,2,2,2,14,4,2,16,256]{8,7,6,5,4,3,2,1,0:T(8,128)(2,1)}, bf16[8,128,1792]{2,1,0:T(8,128)(2,1)}, s32[8,4,14]{2,1,0:T(4,128)}, bf16[2,28,16,128]{3,2,1,0:T(8,128)(2,1)}) custom-call(bf16[1024,1024]{1,0:T(8,128)(2,1)} %refs_0_.1, bf16[2,28,16,128]{3,2,1,0:T(8,128)(2,1)} %bitcast.14, ...), custom_call_target="tpu_custom_call" | custom-call | tf_op jit(solution)/shard_map/gather/pallas_call | solution.py:258
  142.5 0.0 copy-start
  142.5 22.2 %tokens.1 = (bf16[128,14336]{1,0:T(8,128)(2,1)}, bf16[128,8192]{1,0:T(8,128)(2,1)}) custom-call(s32[1]{0:T(128)} %bitcast.me_ref, s32[8,4,14]{2,1,0:T(4,128)} %get-tuple-element.10.br_ref, bf16[64,128,128]{2,1,0:T(8,128)(2,1)} %get-tuple-element.11.tok_ref, bf16[8,4,14,128,256]{4,3,2,1,0:T(8,128)(2,1)} %bitcast.12, ...), custom_call_target="tpu_custom_call" | custom-call | tf_op jit(solution)/shard_map/tokens/pallas_call | solution.py:362
  164.8 0.0 copy-done
  164.8 0.7 copy.8
Async XLA Ops:
  142.5 22.2 %copy-start = (bf16[2,28,16,128]{3,2,1,0:T(8,128)(2,1)S(1)}, bf16[2,28,16,128]{3,2,1,0:T(8,128)(2,1)}, u32[]{:S(2)}) copy-start(bf16[2,28,16,128]{3,2,1,0:T(8,128)(2,1)} %get-tuple-element.16) | copy-start | bytes 688132

commit v2 on v1

--- a/solution.py
+++ b/solution.py
@@ -8,7 +8,7 @@
 MESH = pl.DeviceIdType.MESH
 BF, F32 = jnp.bfloat16, jnp.float32
 HBM = pl.BlockSpec(memory_space=pltpu.HBM)
-WIRES, LOCALS = 88, 24
+WIRES, LOCALS = 89, 24
 VMEM = pl.BlockSpec(memory_space=pltpu.VMEM)
 
 
@@ -183,7 +183,7 @@
     slab[:, :, :, 128:] = upper.reshape(2, 14, 16, 128)
     ystage = [
         go(slab, wide.at[(y + 4 - v) % 4, core, e, :, :, x, zh], at(x, z, v, core))
-        for v in (yp, ym, y2)
+        for v in (yp, ym)
     ]
     placed = lcopy(slab, wide.at[0, core, e, :, :, x, zh])
     early = [go(slab.at[0], wide.at[0, core, e, 0, :, x, zh], p) for p in x_peers]
@@ -192,6 +192,12 @@
     got(*early)
     second = [same(wide.at[0, core, e, 0, :, :, zh], p) for p in z_peers]
     second += [same(wide.at[0, core, :, 1, :, x], p) for p in x_peers]
+    got(*ystage)
+    far = [(3, 0, up), (1, 1, down)]
+    ystage = [
+        go(wide.at[v, core, e, hf, :, x, zh], wide.at[2, core, e, hf, :, x, zh], p)
+        for v, hf, p in far
+    ]
     got(*ystage)
     others = pl.ds(1, 3)
     first = [same(wide.at[others, core, e, 0, :, x, zh], p) for p in x_peers]

time: 166 us -> 165 us (level)
  no operation moved by 1% of the time
where the time goes in v2:
time: 165 us
  Pallas kernels  164 us (99%)
    pallas_call x1, Pallas kernels, gather_all(): pl.pallas_call(gather_body, out_shape=(jax.ShapeDtypeStruct((64, 128, 128...  141 us
    pallas_call x1, Pallas kernels, own_tokens(): pl.pallas_call(tokens_kernel, out_shape=(jax.ShapeDtypeStruct((128, 14336...  22.2 us

profile of v2, /device:TPU:0, one launch (start us, length us, event | category | flops | bytes accessed | tf_op | source)
XLA Modules:
  0.0 164.9 jit_solution(2560909748405673776)
XLA Ops:
  0.6 141.3 %gather.1 = (bf16[64,128,128]{2,1,0:T(8,128)(2,1)}, bf16[4,2,2,2,14,4,2,16,256]{8,7,6,5,4,3,2,1,0:T(8,128)(2,1)}, bf16[8,128,1792]{2,1,0:T(8,128)(2,1)}, s32[8,4,14]{2,1,0:T(4,128)}, bf16[2,28,16,128]{3,2,1,0:T(8,128)(2,1)}) custom-call(bf16[1024,1024]{1,0:T(8,128)(2,1)} %refs_0_.1, bf16[2,28,16,128]{3,2,1,0:T(8,128)(2,1)} %bitcast.14, ...), custom_call_target="tpu_custom_call" | custom-call | tf_op jit(solution)/shard_map/gather/pallas_call | solution.py:264
  142.0 0.0 copy-start
  142.0 22.2 %tokens.1 = (bf16[128,14336]{1,0:T(8,128)(2,1)}, bf16[128,8192]{1,0:T(8,128)(2,1)}) custom-call(s32[1]{0:T(128)} %bitcast.me_ref, s32[8,4,14]{2,1,0:T(4,128)} %get-tuple-element.10.br_ref, bf16[64,128,128]{2,1,0:T(8,128)(2,1)} %get-tuple-element.11.tok_ref, bf16[8,4,14,128,256]{4,3,2,1,0:T(8,128)(2,1)} %bitcast.12, ...), custom_call_target="tpu_custom_call" | custom-call | tf_op jit(solution)/shard_map/tokens/pallas_call | solution.py:368
  164.2 0.0 copy-done
  164.2 0.7 copy.8
Async XLA Ops:
  142.0 22.2 %copy-start = (bf16[2,28,16,128]{3,2,1,0:T(8,128)(2,1)S(1)}, bf16[2,28,16,128]{3,2,1,0:T(8,128)(2,1)}, u32[]{:S(2)}) copy-start(bf16[2,28,16,128]{3,2,1,0:T(8,128)(2,1)} %get-tuple-element.16) | copy-start | bytes 688132

commit v3 on v2

--- a/solution.py
+++ b/solution.py
@@ -154,18 +154,9 @@
 
     def forward_tokens(r, sends, shares):
         got(*sends)
+        forwards = [same(half_shard(r, ym, 0), up), same(half_shard(r, yp, 1), down)]
         shares += [same(shard(r, v, core), sib) for v in (ym, yp)]
-        return [same(half_shard(r, ym, 0), up), same(half_shard(r, yp, 1), down)]
-
-    def finish_tokens(r, shares, forwards):
-        got(*forwards)
-        last = same(shard(r, y2, core), sib)
-        if r == 1:
-            sent(*forwards)
-            for c, p in zip(cols, col_peers):
-                go(gh_ref.at[pl.ds(pl.multiple_of(c * 128, 128), 128)], ghb.at[col], p)
-        got(*shares)
-        got(last)
+        return forwards
 
     for c in own_tok[0]:
         c.wait()
@@ -226,8 +217,10 @@
     own_copy.wait()
     same(wide.at[0, core], sib)
 
-    finish_tokens(0, shares0, forwards0)
+    got(*forwards0)
+    shares0.append(same(shard(0, y2, core), sib))
     forwards1 = forward_tokens(1, sends1, shares1)
+    got(*shares0)
     own_gh.wait()
     terms = (rows_ref, tok[0], own_w, gh, picked, grads, acc, dw)
     weight_terms(0, (0, 14), *terms)
@@ -238,7 +231,12 @@
     for part in (w0(zm, every), w0(zp, every), w1(xm, every), w1(xp, every)):
         same(part, sib)
 
-    finish_tokens(1, shares1, forwards1)
+    got(*forwards1)
+    shares1.append(same(shard(1, y2, core), sib))
+    sent(*forwards1)
+    for c, p in zip(cols, col_peers):
+        go(gh_ref.at[pl.ds(pl.multiple_of(c * 128, 128), 128)], ghb.at[col], p)
+    got(*shares1)
     rows_at = pl.ds(pl.multiple_of(col % 4 * 128, 128), 128)
     keep = [pltpu.make_async_copy(t.at[:, rows_at], tokb, local.at[LOCALS - 1]) for t in tok]
     for h in range(2):

time: 165 us -> 165 us (level)
  no operation moved by 1% of the time
where the time goes in v3:
time: 165 us
  Pallas kernels  164 us (99%)
    pallas_call x1, Pallas kernels, gather_all(): pl.pallas_call(gather_body, out_shape=(jax.ShapeDtypeStruct((64, 128, 128...  141 us
    pallas_call x1, Pallas kernels, own_tokens(): pl.pallas_call(tokens_kernel, out_shape=(jax.ShapeDtypeStruct((128, 14336...  22.2 us

profile of v3, /device:TPU:0, one launch (start us, length us, event | category | flops | bytes accessed | tf_op | source)
XLA Modules:
  0.0 164.9 jit_solution(1754116351668362463)
XLA Ops:
  0.6 141.3 %gather.1 = (bf16[64,128,128]{2,1,0:T(8,128)(2,1)}, bf16[4,2,2,2,14,4,2,16,256]{8,7,6,5,4,3,2,1,0:T(8,128)(2,1)}, bf16[8,128,1792]{2,1,0:T(8,128)(2,1)}, s32[8,4,14]{2,1,0:T(4,128)}, bf16[2,28,16,128]{3,2,1,0:T(8,128)(2,1)}) custom-call(bf16[1024,1024]{1,0:T(8,128)(2,1)} %refs_0_.1, bf16[2,28,16,128]{3,2,1,0:T(8,128)(2,1)} %bitcast.14, ...), custom_call_target="tpu_custom_call" | custom-call | tf_op jit(solution)/shard_map/gather/pallas_call | solution.py:262
  142.0 0.0 copy-start
  142.0 22.2 %tokens.1 = (bf16[128,14336]{1,0:T(8,128)(2,1)}, bf16[128,8192]{1,0:T(8,128)(2,1)}) custom-call(s32[1]{0:T(128)} %bitcast.me_ref, s32[8,4,14]{2,1,0:T(4,128)} %get-tuple-element.10.br_ref, bf16[64,128,128]{2,1,0:T(8,128)(2,1)} %get-tuple-element.11.tok_ref, bf16[8,4,14,128,256]{4,3,2,1,0:T(8,128)(2,1)} %bitcast.12, ...), custom_call_target="tpu_custom_call" | custom-call | tf_op jit(solution)/shard_map/tokens/pallas_call | solution.py:366
  164.2 0.0 copy-done
  164.2 0.7 copy.8
Async XLA Ops:
  142.0 22.2 %copy-start = (bf16[2,28,16,128]{3,2,1,0:T(8,128)(2,1)S(1)}, bf16[2,28,16,128]{3,2,1,0:T(8,128)(2,1)}, u32[]{:S(2)}) copy-start(bf16[2,28,16,128]{3,2,1,0:T(8,128)(2,1)} %get-tuple-element.16) | copy-start | bytes 688132
